TPU v7x, 256 devices: a whole 4x4x8 slice. The times are simulated.
256 devices in a mesh: hist: 64 (over z, y, core), mp: 4 (over x).
Axes of the slice: x: 4, y: 4, z: 8, core: 2. Of those that a mesh axis runs over, the one named last changes fastest.
Arguments:
- candidates: bfloat16 [65536, 1024], P('hist'), may hold values from -6 to 6
- w_gate: bfloat16 [1024, 1024], P(None, 'mp'), may hold values from -0.1875 to 0.1875
- w_query: bfloat16 [1024, 1024], P(None, 'mp'), may hold values from -0.1875 to 0.1875
- w_out: bfloat16 [1024, 1024], replicated, may hold values from -0.1875 to 0.1875
- gain: float32 [1024], P('mp'), may hold values from 0.1 to 1.9
- key_cache: bfloat16 [128, 3072, 1024], P('hist', None, 'mp'), may hold values from -6 to 6
- value_cache: bfloat16 [128, 3072, 1024], P('hist', None, 'mp'), may hold values from -6 to 6
- hist_blocks: int32 [128], P('hist'), may hold values from 12 to 24
- request_owner: int32 [4096, 1], P('hist'), may hold values from 0 to 63; in each aligned block of 64 rows (0 to 63, 64 to 127, ...) at most 2 rows name the same one
- request_slot: int32 [4096], P('hist'), may hold values from 0 to 1
- block_offsets: int32 [4096, 12], P('hist'), may hold values from 0 to 11
Outputs:
- scored: bfloat16 [65536, 1024], P('hist', 'mp')
Inputs may be any that keep to these rules, and one draw needn't show every extreme that they name: `request_owner`: among the 64 requests of one index of hist, at most 2 name the same owner, a bound that some block reaches.
All inputs are finite; a program needn't handle non-finite values.
Results may differ from a plain program's by a relative error of at most 0.007.
Values may be sent and summed in bfloat16 or wider, within the bound.
A program may use at most 64 MiB of HBM per device.

v0:
```python
import math

import jax
import jax.numpy as jnp
from jax import lax
from jax.sharding import PartitionSpec as P

DH = 128
BLK = 128
HBLK = 24


def on_device(
    candidates,
    w_gate,
    w_query,
    w_out,
    gain,
    key_cache,
    value_cache,
    hist_blocks,
    request_owner,
    request_slot,
    block_offsets,
):
    gate_u = jax.nn.silu(jnp.dot(candidates, w_gate, preferred_element_type=jnp.float32))
    query = jax.nn.silu(jnp.dot(candidates, w_query, preferred_element_type=jnp.float32)).astype(
        jnp.bfloat16
    )
    req_count = request_slot.shape[0]
    cand_rows = candidates.shape[0] // req_count
    local_width = query.shape[1]
    local_heads = local_width // DH
    hist_count = lax.axis_size("hist")
    capacity = max(2, 2 * req_count // hist_count)
    slot_count = hist_count * capacity
    owners = request_owner[:, 0]
    order = jnp.arange(req_count, dtype=jnp.int32)
    same_owner = owners[None, :] == owners[:, None]
    earlier = order[None, :] < order[:, None]
    rank = jnp.sum(jnp.where(same_owner & earlier, 1, 0), axis=1).astype(jnp.int32)
    target = owners * capacity + rank
    placing = jnp.arange(slot_count, dtype=jnp.int32)[:, None] == target[None, :]
    placing_bf = placing.astype(jnp.bfloat16)
    query_flat = query.reshape(req_count, cand_rows * local_width)
    send_query = jnp.dot(placing_bf, query_flat, preferred_element_type=jnp.float32).astype(
        jnp.bfloat16
    )
    send_query = send_query.reshape(hist_count, capacity, cand_rows, local_width)
    request_info = jnp.concatenate([request_slot[:, None], block_offsets], axis=1)
    send_info = jnp.sum(jnp.where(placing[:, :, None], request_info[None, :, :], 0), axis=1)
    send_info = send_info.reshape(hist_count, capacity, request_info.shape[1])
    users_here = hist_blocks.shape[0]
    window = HBLK // 2
    window_events = window * BLK
    key_parts = []
    value_parts = []
    for user_index in range(users_here):
        first = (hist_blocks[user_index] - window) * BLK
        key_parts.append(lax.dynamic_slice_in_dim(key_cache[user_index], first, window_events, 0))
        value_parts.append(
            lax.dynamic_slice_in_dim(value_cache[user_index], first, window_events, 0)
        )
    all_events = users_here * window_events
    window_keys = jnp.concatenate(key_parts, axis=0).reshape(all_events, local_heads, DH)
    window_values = jnp.concatenate(value_parts, axis=0).reshape(all_events, local_heads, DH)
    scale = DH ** (-0.5)
    got_query = lax.all_to_all(send_query, "hist", split_axis=0, concat_axis=0, tiled=True)
    got_info = lax.all_to_all(send_info, "hist", split_axis=0, concat_axis=0, tiled=True)
    items = got_query.shape[1]
    total = hist_count * items
    picks = got_info.shape[2] - 1
    flat_query = got_query.reshape(total, cand_rows, local_heads, DH)
    flat_info = got_info.reshape(total, picks + 1)
    user_slot = flat_info[:, 0]
    offsets = flat_info[:, 1:]
    block_slot = window - 1 - jnp.arange(window, dtype=jnp.int32)
    hits = jnp.sum(jnp.where(offsets[:, :, None] == block_slot[None, None, :], 1.0, 0.0), axis=1)
    match_user = user_slot[:, None] == jnp.arange(users_here, dtype=jnp.int32)[None, :]
    multiple = jnp.where(match_user[:, :, None], hits[:, None, :], 0.0).astype(jnp.float32)
    multiple = multiple.reshape(total, users_here * window)
    group = math.gcd(total, 16)
    grouped_query = flat_query.reshape(total // group, group, cand_rows, local_heads, DH)
    grouped_multiple = multiple.reshape(total // group, group, users_here * window)

    def attend_group(pair):
        query_group, multiple_group = pair
        scores = (
            jnp.einsum(
                "gchd,khd->ghck", query_group, window_keys, preferred_element_type=jnp.float32
            )
            * scale
        )
        weights = jax.nn.silu(scores).astype(jnp.bfloat16).astype(jnp.float32)
        weights = weights.reshape(group, local_heads, cand_rows, users_here * window, BLK)
        counted = weights * multiple_group[:, None, None, :, None]
        upper = counted.astype(jnp.bfloat16)
        lower = (counted - upper.astype(jnp.float32)).astype(jnp.bfloat16)
        upper = upper.reshape(group, local_heads, cand_rows, all_events)
        lower = lower.reshape(group, local_heads, cand_rows, all_events)
        result = jnp.einsum(
            "ghck,khd->gchd", upper, window_values, preferred_element_type=jnp.float32
        )
        result = result + jnp.einsum(
            "ghck,khd->gchd", lower, window_values, preferred_element_type=jnp.float32
        )
        return result.astype(jnp.bfloat16)

    outcome = lax.map(attend_group, (grouped_query, grouped_multiple))
    outcome = outcome.reshape(hist_count, items, cand_rows, local_width)
    answers = lax.all_to_all(outcome, "hist", split_axis=0, concat_axis=0, tiled=True)
    answers_flat = answers.reshape(slot_count, cand_rows * local_width)
    attended = jnp.dot(placing_bf.T, answers_flat, preferred_element_type=jnp.float32).astype(
        jnp.bfloat16
    )
    attended = attended.reshape(req_count * cand_rows, local_width)
    widened = attended.astype(jnp.float32)
    full_width = local_width * lax.axis_size("mp")
    row_sum, row_squares = lax.psum(
        (jnp.sum(widened, axis=-1), jnp.sum(widened * widened, axis=-1)), "mp"
    )
    mean = row_sum / full_width
    var = row_squares / full_width - mean * mean
    normed = (widened - mean[:, None]) / jnp.sqrt(var[:, None] + 1e-05)
    gated = (normed * gain[None, :] * gate_u).astype(jnp.bfloat16)
    quarter = candidates.shape[1] // lax.axis_size("mp")
    col_start = lax.axis_index("mp") * quarter
    residual = lax.dynamic_slice_in_dim(candidates, col_start, quarter, 1).astype(jnp.float32)
    row_start = lax.axis_index("mp") * local_width
    weight_rows = lax.dynamic_slice_in_dim(w_out, row_start, local_width, 0)
    partial_out = jnp.dot(gated, weight_rows, preferred_element_type=jnp.float32)
    mine = lax.psum_scatter(partial_out, "mp", scatter_dimension=1, tiled=True)
    return (mine + residual).astype(jnp.bfloat16)


def solution(mesh):
    in_specs = (
        P("hist", None),
        P(None, "mp"),
        P(None, "mp"),
        P(),
        P("mp"),
        P("hist", None, "mp"),
        P("hist", None, "mp"),
        P("hist"),
        P("hist", None),
        P("hist"),
        P("hist", None),
    )
    out_specs = P("hist", "mp")
    return jax.shard_map(
        on_device, mesh=mesh, in_specs=in_specs, out_specs=out_specs, check_vma=False
    )
```

profile of v0, /device:TPU:1, one launch (start us, length us, event | category | flops | bytes accessed | tf_op | source)
XLA Modules:
  0.0 259.2 jit_solution(12361914496453158869)
XLA Ops:
  9.9 13.2 %all-to-all-start.1 = ((s32[64,2,13]{2,1,0:T(2,128)}), s32[64,2,13]{2,1,0:T(2,128)S(1)}, u32[]{:S(2)}, u32[]{:S(2)}) async-start(s32[64,2,13]{2,1,0:T(2,128)} %bitcast.16), calls=%async_computation.1 | async-start | bytes 131072 | tf_op jit(solution)/shard_map/all_to_all | solution.py:69
  25.8 3.8 %fusion.35 = (bf16[1,3072,256]{2,1,0:T(8,128)(2,1)}, bf16[1,3072,256]{2,1,0:T(8,128)(2,1)}) fusion(bf16[2,3072,256]{2,1,0:T(8,128)(2,1)} %param.19), kind=kLoop, calls=%fused_computation.62 | loop fusion | bytes 6291456 | tf_op jit(solution)/shard_map/slice | solution.py:62
  29.6 2.6 %constant_dynamic-slice_fusion.1 = (bf16[1,1536,256]{2,1,0:T(8,128)(2,1)}, bf16[1,1536,256]{2,1,0:T(8,128)(2,1)}) fusion(bf16[1,3072,256]{2,1,0:T(8,128)(2,1)} %get-tuple-element.73, s32[]{:T(128)S(6)} %select_n.34, bf16[1,3072,256]{2,1,0:T(8,128)(2,1)} %get-tuple-element.72, s32[]{:T(128)S(6)} %select_n.33), kind=kLoop, calls=%fused_computation.53 | loop fusion | bytes 3145736 | tf_op jit(solution)/shard_map/dynamic_slice | solution.py:62
  33.6 2.3 copy.57
  35.9 3.2 %multiply_convert_fusion.1 = bf16[1024,256]{1,0:T(8,128)(2,1)} fusion(bf16[1024,1024]{1,0:T(8,128)(2,1)} %param.13, bf16[1024,256]{1,0:T(8,128)(2,1)} %param.15), kind=kOutput, calls=%fused_computation.32 | convolution fusion | flops 538181632 | bytes 3145728 | tf_op jit(solution)/shard_map/dot_general | solution.py:27
  39.1 2.1 reshape.116
  41.2 2.5 pad_maximum_fusion.1
  44.2 2.6 %copy.43 = bf16[3072,2,128]{2,0,1:T(8,128)(2,1)} copy(bf16[3072,2,128]{0,2,1:T(8,128)(2,1)} %pad_maximum_fusion.1) | data formatting | bytes 3145728 | tf_op jit(solution)/shard_map/while | solution.py:109
  48.1 10.3 %all-to-all-start = ((bf16[64,2,16,256]{3,2,1,0:T(8,128)(2,1)}), bf16[64,2,16,256]{3,2,1,0:T(8,128)(2,1)S(1)}, u32[]{:S(2)}, u32[]{:S(2)}) async-start(bf16[64,2,16,256]{3,2,1,0:T(8,128)(2,1)} %bitcast.26), calls=%async_computation | async-start | bytes 2097152 | tf_op jit(solution)/shard_map/all_to_all | solution.py:68
  58.4 2.1 fusion.36
  61.7 2.3 copy.51
  64.0 2.3 copy.53
  66.3 2.7 %pad_maximum_fusion = bf16[3072,2,128]{0,2,1:T(8,128)(2,1)} fusion(bf16[1536,2,128]{0,2,1:T(8,128)(2,1)} %bitcast.98, bf16[1536,2,128]{0,2,1:T(8,128)(2,1)} %bitcast.97), kind=kLoop, calls=%fused_computation.27 | loop fusion | flops 3145728 | bytes 3145728 | tf_op jit(solution)/shard_map/concatenate | solution.py:65
  69.0 2.6 copy.41
  72.2 14.2 %all-to-all-done = bf16[64,2,16,256]{3,2,1,0:T(8,128)(2,1)S(1)} async-done(((bf16[64,2,16,256]{3,2,1,0:T(8,128)(2,1)}), bf16[64,2,16,256]{3,2,1,0:T(8,128)(2,1)S(1)}, u32[]{:S(2)}, u32[]{:S(2)}) %all-to-all-start) | async-done | bytes 1048608 | tf_op jit(solution)/shard_map/all_to_all | solution.py:68
  87.5 60.7 %while.10 = (s32[]{:T(128)}, bf16[8,16,16,2,128]{4,3,2,1,0:T(2,128)(2,1)}, bf16[8,16,16,2,128]{4,3,2,1,0:T(2,128)(2,1)}, bf16[3072,2,128]{2,0,1:T(8,128)(2,1)}, ...) while((s32[]{:T(128)}, bf16[8,16,16,2,128]{4,3,2,1,0:T(2,128)(2,1)}, ...), condition=%wide.region_4.5_spmd, body=%wide.region_3.4_spmd.sunk | while | flops 1231683584 | bytes 22746224 | solution.py:109
  88.5 3.5 %fusion.57 = bf16[16,2,16,3072]{3,2,0,1:T(8,128)(2,1)S(1)} fusion(bf16[3072,2,128]{2,0,1:T(8,128)(2,1)} %get-tuple-element.138, bf16[1,16,16,2,128]{4,3,2,1,0:T(2,128)(2,1)S(1)} %constant_dynamic-slice_fusion.6), kind=kOutput, calls=%fused_computation.8.clone.1 | convolution fusion | flops 412090368 | bytes 4849664 | tf_op jit(solution)/shard_map/while/body/eval_jaxpr/gchd,khd->ghck/dot_general | solution.py:89
  96.1 3.5 %fusion.57 = bf16[16,2,16,3072]{3,2,0,1:T(8,128)(2,1)S(1)} fusion(bf16[3072,2,128]{2,0,1:T(8,128)(2,1)} %get-tuple-element.138, bf16[1,16,16,2,128]{4,3,2,1,0:T(2,128)(2,1)S(1)} %constant_dynamic-slice_fusion.6), kind=kOutput, calls=%fused_computation.8.clone.1 | convolution fusion | flops 412090368 | bytes 4849664 | tf_op jit(solution)/shard_map/while/body/eval_jaxpr/gchd,khd->ghck/dot_general | solution.py:89
  103.7 3.5 %fusion.57 = bf16[16,2,16,3072]{3,2,0,1:T(8,128)(2,1)S(1)} fusion(bf16[3072,2,128]{2,0,1:T(8,128)(2,1)} %get-tuple-element.138, bf16[1,16,16,2,128]{4,3,2,1,0:T(2,128)(2,1)S(1)} %constant_dynamic-slice_fusion.6), kind=kOutput, calls=%fused_computation.8.clone.1 | convolution fusion | flops 412090368 | bytes 4849664 | tf_op jit(solution)/shard_map/while/body/eval_jaxpr/gchd,khd->ghck/dot_general | solution.py:89
  111.2 3.5 %fusion.57 = bf16[16,2,16,3072]{3,2,0,1:T(8,128)(2,1)S(1)} fusion(bf16[3072,2,128]{2,0,1:T(8,128)(2,1)} %get-tuple-element.138, bf16[1,16,16,2,128]{4,3,2,1,0:T(2,128)(2,1)S(1)} %constant_dynamic-slice_fusion.6), kind=kOutput, calls=%fused_computation.8.clone.1 | convolution fusion | flops 412090368 | bytes 4849664 | tf_op jit(solution)/shard_map/while/body/eval_jaxpr/gchd,khd->ghck/dot_general | solution.py:89
  118.8 3.5 %fusion.57 = bf16[16,2,16,3072]{3,2,0,1:T(8,128)(2,1)S(1)} fusion(bf16[3072,2,128]{2,0,1:T(8,128)(2,1)} %get-tuple-element.138, bf16[1,16,16,2,128]{4,3,2,1,0:T(2,128)(2,1)S(1)} %constant_dynamic-slice_fusion.6), kind=kOutput, calls=%fused_computation.8.clone.1 | convolution fusion | flops 412090368 | bytes 4849664 | tf_op jit(solution)/shard_map/while/body/eval_jaxpr/gchd,khd->ghck/dot_general | solution.py:89
  126.4 3.6 %fusion.57 = bf16[16,2,16,3072]{3,2,0,1:T(8,128)(2,1)S(1)} fusion(bf16[3072,2,128]{2,0,1:T(8,128)(2,1)} %get-tuple-element.138, bf16[1,16,16,2,128]{4,3,2,1,0:T(2,128)(2,1)S(1)} %constant_dynamic-slice_fusion.6), kind=kOutput, calls=%fused_computation.8.clone.1 | convolution fusion | flops 412090368 | bytes 4849664 | tf_op jit(solution)/shard_map/while/body/eval_jaxpr/gchd,khd->ghck/dot_general | solution.py:89
  134.0 3.5 %fusion.57 = bf16[16,2,16,3072]{3,2,0,1:T(8,128)(2,1)S(1)} fusion(bf16[3072,2,128]{2,0,1:T(8,128)(2,1)} %get-tuple-element.138, bf16[1,16,16,2,128]{4,3,2,1,0:T(2,128)(2,1)S(1)} %constant_dynamic-slice_fusion.6), kind=kOutput, calls=%fused_computation.8.clone.1 | convolution fusion | flops 412090368 | bytes 4849664 | tf_op jit(solution)/shard_map/while/body/eval_jaxpr/gchd,khd->ghck/dot_general | solution.py:89
  141.6 3.6 %fusion.57 = bf16[16,2,16,3072]{3,2,0,1:T(8,128)(2,1)S(1)} fusion(bf16[3072,2,128]{2,0,1:T(8,128)(2,1)} %get-tuple-element.138, bf16[1,16,16,2,128]{4,3,2,1,0:T(2,128)(2,1)S(1)} %constant_dynamic-slice_fusion.6), kind=kOutput, calls=%fused_computation.8.clone.1 | convolution fusion | flops 412090368 | bytes 4849664 | tf_op jit(solution)/shard_map/while/body/eval_jaxpr/gchd,khd->ghck/dot_general | solution.py:89
  148.2 2.5 reshape.120
  150.7 6.5 %all-to-all-start.2 = ((bf16[64,2,16,256]{3,2,1,0:T(8,128)(2,1)}), bf16[64,2,16,256]{3,2,1,0:T(8,128)(2,1)S(1)}, u32[]{:S(2)}, u32[]{:S(2)}) async-start(bf16[64,2,16,256]{3,2,1,0:T(8,128)(2,1)} %reshape.120), calls=%async_computation.2 | async-start | bytes 2097152 | tf_op jit(solution)/shard_map/all_to_all | solution.py:111
  157.2 27.9 %all-to-all-done.2 = bf16[64,2,16,256]{3,2,1,0:T(8,128)(2,1)S(1)} async-done(((bf16[64,2,16,256]{3,2,1,0:T(8,128)(2,1)}), bf16[64,2,16,256]{3,2,1,0:T(8,128)(2,1)S(1)}, u32[]{:S(2)}, u32[]{:S(2)}) %all-to-all-start.2) | async-done | bytes 1048608 | tf_op jit(solution)/shard_map/all_to_all | solution.py:111
  187.1 1.6 fusion.34
  188.7 8.6 %all-reduce = (f32[1024]{0:T(1024)S(1)}, f32[1024]{0:T(1024)S(1)}) all-reduce(f32[1024]{0:T(1024)S(1)} %get-tuple-element.57, f32[1024]{0:T(1024)S(1)} %get-tuple-element.56), channel_id=1, replica_groups=mesh['hist'=64,'mp'=4] {'mp'}, use_global_device_ids=true, to_apply=%region_8.9 | all-reduce | flops 2048 | bytes 16384 | tf_op jit(solution)/shard_map/psum | solution.py:119
  197.3 6.2 %fusion.23 = f32[1024,1024]{1,0:T(8,128)} fusion(f32[1024,256]{1,0:T(8,128)} %reshape.122, bf16[1024,1024]{1,0:T(8,128)(2,1)S(1)} %copy-done, s32[]{:T(128)S(6)} %select_n.39, f32[256]{0:T(256)S(1)} %copy-done.3, f32[1024]{0:T(1024)S(1)} %get-tuple-element.77, f32[1024]{0:T(1024)S(1)} %get-tuple-element.76, bf16[1024,1024]{1,0:T(8,128)(2,1)} %param.13, ...), kind=kOutput, calls=%fused_computation.33 | convolution fusion | flops 1076101120 | bytes 8397828 | tf_op jit(solution)/shard_map/dot_general | solution.py:131
  203.5 46.5 %reduce-scatter.2.cloned.1.call-done = f32[1024,256]{1,0:T(8,128)} async-done(((f32[1024,1024]{1,0:T(8,128)}), f32[1024,256]{1,0:T(8,128)}) %reduce-scatter.2.cloned.1.call-update) | async-done | bytes 1048592 | tf_op jit(solution)/shard_map/reduce_scatter | solution.py:132
  250.1 2.3 add_convert_fusion
  (107 shorter events, 44.7 us)
Async XLA Ops:
  6.5 190.7 %copy-start = (bf16[1024,1024]{1,0:T(8,128)(2,1)S(1)}, bf16[1024,1024]{1,0:T(8,128)(2,1)}, u32[]{:S(2)}) copy-start(bf16[1024,1024]{1,0:T(8,128)(2,1)} %param.16) | copy-start | bytes 6291460
  9.9 38.2 %all-to-all-start.1 = ((s32[64,2,13]{2,1,0:T(2,128)}), s32[64,2,13]{2,1,0:T(2,128)S(1)}, u32[]{:S(2)}, u32[]{:S(2)}) async-start(s32[64,2,13]{2,1,0:T(2,128)} %bitcast.16), calls=%async_computation.1 | async-start | bytes 131072 | tf_op jit(solution)/shard_map/all_to_all | solution.py:69
  41.1 2.5 copy-start.1
  48.1 38.3 %all-to-all-start = ((bf16[64,2,16,256]{3,2,1,0:T(8,128)(2,1)}), bf16[64,2,16,256]{3,2,1,0:T(8,128)(2,1)S(1)}, u32[]{:S(2)}, u32[]{:S(2)}) async-start(bf16[64,2,16,256]{3,2,1,0:T(8,128)(2,1)} %bitcast.26), calls=%async_computation | async-start | bytes 2097152 | tf_op jit(solution)/shard_map/all_to_all | solution.py:68
  88.5 3.7 %copy-start.2 = (bf16[3072,2,128]{2,0,1:T(8,128)(2,1)S(1)}, bf16[3072,2,128]{2,0,1:T(8,128)(2,1)}, u32[]{:S(2)}) copy-start(bf16[3072,2,128]{2,0,1:T(8,128)(2,1)} %get-tuple-element.140) | copy-start | bytes 4718596 | tf_op jit(solution)/shard_map/while
  96.1 3.7 %copy-start.2 = (bf16[3072,2,128]{2,0,1:T(8,128)(2,1)S(1)}, bf16[3072,2,128]{2,0,1:T(8,128)(2,1)}, u32[]{:S(2)}) copy-start(bf16[3072,2,128]{2,0,1:T(8,128)(2,1)} %get-tuple-element.140) | copy-start | bytes 4718596 | tf_op jit(solution)/shard_map/while
  103.6 3.7 %copy-start.2 = (bf16[3072,2,128]{2,0,1:T(8,128)(2,1)S(1)}, bf16[3072,2,128]{2,0,1:T(8,128)(2,1)}, u32[]{:S(2)}) copy-start(bf16[3072,2,128]{2,0,1:T(8,128)(2,1)} %get-tuple-element.140) | copy-start | bytes 4718596 | tf_op jit(solution)/shard_map/while
  111.2 3.7 %copy-start.2 = (bf16[3072,2,128]{2,0,1:T(8,128)(2,1)S(1)}, bf16[3072,2,128]{2,0,1:T(8,128)(2,1)}, u32[]{:S(2)}) copy-start(bf16[3072,2,128]{2,0,1:T(8,128)(2,1)} %get-tuple-element.140) | copy-start | bytes 4718596 | tf_op jit(solution)/shard_map/while
  118.8 3.7 %copy-start.2 = (bf16[3072,2,128]{2,0,1:T(8,128)(2,1)S(1)}, bf16[3072,2,128]{2,0,1:T(8,128)(2,1)}, u32[]{:S(2)}) copy-start(bf16[3072,2,128]{2,0,1:T(8,128)(2,1)} %get-tuple-element.140) | copy-start | bytes 4718596 | tf_op jit(solution)/shard_map/while
  126.4 3.8 %copy-start.2 = (bf16[3072,2,128]{2,0,1:T(8,128)(2,1)S(1)}, bf16[3072,2,128]{2,0,1:T(8,128)(2,1)}, u32[]{:S(2)}) copy-start(bf16[3072,2,128]{2,0,1:T(8,128)(2,1)} %get-tuple-element.140) | copy-start | bytes 4718596 | tf_op jit(solution)/shard_map/while
  134.0 3.7 %copy-start.2 = (bf16[3072,2,128]{2,0,1:T(8,128)(2,1)S(1)}, bf16[3072,2,128]{2,0,1:T(8,128)(2,1)}, u32[]{:S(2)}) copy-start(bf16[3072,2,128]{2,0,1:T(8,128)(2,1)} %get-tuple-element.140) | copy-start | bytes 4718596 | tf_op jit(solution)/shard_map/while
  141.6 3.8 %copy-start.2 = (bf16[3072,2,128]{2,0,1:T(8,128)(2,1)S(1)}, bf16[3072,2,128]{2,0,1:T(8,128)(2,1)}, u32[]{:S(2)}) copy-start(bf16[3072,2,128]{2,0,1:T(8,128)(2,1)} %get-tuple-element.140) | copy-start | bytes 4718596 | tf_op jit(solution)/shard_map/while
  150.7 34.5 %all-to-all-start.2 = ((bf16[64,2,16,256]{3,2,1,0:T(8,128)(2,1)}), bf16[64,2,16,256]{3,2,1,0:T(8,128)(2,1)S(1)}, u32[]{:S(2)}, u32[]{:S(2)}) async-start(bf16[64,2,16,256]{3,2,1,0:T(8,128)(2,1)} %reshape.120), calls=%async_computation.2 | async-start | bytes 2097152 | tf_op jit(solution)/shard_map/all_to_all | solution.py:111
  157.2 92.9 %reduce-scatter.2.cloned.1.call-start = ((), (), s32[]{:S(2)}) async-start(), calls=%async_computation.4 | async-start | bytes 5242880 | tf_op jit(solution)/shard_map/reduce_scatter | solution.py:132
  185.9 11.3 %copy-start.3 = (f32[256]{0:T(256)S(1)}, f32[256]{0:T(256)}, u32[]{:S(2)}) copy-start(f32[256]{0:T(256)} %param.17) | copy-start | bytes 3076
Sparse Core Ops, SparseCore 0:
  203.7 46.3 reduce-scatter.1
where the time goes:
time: 260 us; the launch traced here: 259 us
  waiting for transfers between devices  88.6 us (34%)
  matrix products  54.9 us (21%)
  local copies, waits for them, and re-layouts  49.9 us (19%)
  starting transfers between devices  30 us (12%)
  between operations  14.9 us (6%)
  other arithmetic  11.7 us (4%)
  blocking collectives  8.59 us (3%)
    reduce_scatter x1, waiting for transfers between devices, on_device(): mine = lax.psum_scatter(partial_out, 'mp', scatter_dimension=1, tiled=True)  46.5 us
    dot_general x8, matrix products, attend_group(): jnp.einsum('gchd,khd->ghck', query_group, window_keys, preferred_element_...  28.4 us
    all_to_all x1, waiting for transfers between devices, on_device(): lax.all_to_all(outcome, 'hist', split_axis=0, concat_axis=0, tiled=True)  27.9 us
    all_to_all x1, waiting for transfers between devices, on_device(): lax.all_to_all(send_query, 'hist', split_axis=0, concat_axis=0, tiled=True)  14.2 us
    all_to_all x1, starting transfers between devices, on_device(): lax.all_to_all(send_info, 'hist', split_axis=0, concat_axis=0, tiled=True)  13.2 us
    all_to_all x1, starting transfers between devices, on_device(): lax.all_to_all(send_query, 'hist', split_axis=0, concat_axis=0, tiled=True)  10.3 us
    unnamed x12, local copies, waits for them, and re-layouts  9.98 us
    psum x1, blocking collectives, on_device(): lax.psum((jnp.sum(widened, axis=-1), jnp.sum(widened * widened, axis=-1))...  8.59 us
  transfers between devices with their start and end apart: 4, of which 3 were waited for; matrix products, arithmetic and copies ran while one was open for 14% of the time, Pallas kernels for 0%

commit v1 on v0

v1 whole, which is shorter than its diff:
```python
import jax
import jax.numpy as jnp
from jax import lax
from jax.experimental import pallas as pl
from jax.experimental.pallas import tpu as pltpu
from jax.sharding import PartitionSpec as P

MESH = pl.DeviceIdType.MESH
F32 = jnp.float32
BF16 = jnp.bfloat16

NZ, NY, NC = 8, 4, 2
NH = NZ * NY * NC
CHUNKS, PER = 8, 8
NX = 4
CAP = 2
CAND = 16
REQ = 64
DH = 128
WIN = 12
HBLK = 24
SUB = CAND // NX
ROWS = PER * CAP * CAND
GRP = 4


def step_shift(k):
    chunk, dz = lax.div(k, PER), lax.rem(k, PER)
    low = lax.rem(chunk + dz, PER)
    return dz, lax.div(low, NC), lax.rem(low, NC)


def peer_of(h, k, sign):
    z, y, c = lax.div(h, NY * NC), lax.rem(lax.div(h, NC), NY), lax.rem(h, NC)
    dz, dy, dc = step_shift(k)
    z = lax.rem(z + NZ + sign * dz, NZ)
    y = lax.rem(y + NY + sign * dy, NY)
    c = lax.rem(c + dc, NC)
    return (z * NY + y) * NC + c


def silu(v):
    half = v * 0.5
    return half + half * jnp.tanh(half)


def kernel(
    idx_ref,
    hb_ref,
    mrow_ref,
    tgt_ref,
    gain_ref,
    cand_hbm,
    wq_hbm,
    wg_hbm,
    wo_hbm,
    k_hbm,
    v_hbm,
    out_ref,
    cand_v,
    wq_v,
    wg_v,
    wo_v,
    k_v,
    v_v,
    q_v,
    sendq,
    sendm,
    recvq,
    recvm,
    mexp,
    xs,
    xr,
    ans,
    perm,
    place,
    csub,
    gg,
    gains,
    att,
    outs,
    load_sem,
    fq_send,
    fm_send,
    fq_recv,
    fm_recv,
    w_send,
    w_recv,
    g_send,
    g_recv,
    x_send,
    x_recv,
    a_send,
    a_recv,
    o_send,
    o_recv,
    o_own,
):
    h = lax.axis_index("hist")
    me = lax.axis_index("mp")

    barrier = pltpu.get_barrier_semaphore()

    def greet(k, carry):
        pl.semaphore_signal(
            barrier, inc=1, device_id=(peer_of(h, k, 1), me), device_id_type=MESH
        )
        return carry

    loads = [
        pltpu.make_async_copy(cand_hbm, cand_v, load_sem.at[0]),
        pltpu.make_async_copy(wq_hbm, wq_v, load_sem.at[1]),
        pltpu.make_async_copy(wg_hbm, wg_v.at[me], load_sem.at[2]),
        pltpu.make_async_copy(k_hbm, k_v, load_sem.at[3]),
        pltpu.make_async_copy(v_hbm, v_v, load_sem.at[4]),
    ] + [
        pltpu.make_async_copy(
            wo_hbm.at[:, pl.ds(b * 256, 256)], wo_v.at[b], load_sem.at[5 + b]
        )
        for b in range(NX)
    ]
    for load in loads:
        load.start()
    lax.fori_loop(1, NH, greet, 0)
    for d in range(1, NX):
        pl.semaphore_signal(
            barrier, inc=1, device_id=(h, lax.rem(me + d, NX)), device_id_type=MESH
        )

    loads[0].wait()
    loads[1].wait()

    def project(t, carry):
        acc = jnp.dot(
            cand_v[pl.ds(pl.multiple_of(t * 256, 256), 256), :],
            wq_v[...],
            preferred_element_type=F32,
        )
        q_v[pl.ds(t * 16, 16)] = silu(acc).astype(BF16).reshape(16, CAND, 2 * DH)
        return carry

    lax.fori_loop(0, 4, project, 0)

    pl.semaphore_wait(barrier, NH - 1 + NX - 1)

    def fq_copy(k):
        return pltpu.make_async_remote_copy(
            src_ref=sendq.at[k],
            dst_ref=recvq.at[k],
            send_sem=fq_send,
            recv_sem=fq_recv.at[lax.div(k, PER)],
            device_id=(peer_of(h, k, 1), me),
            device_id_type=MESH,
        )

    def fm_copy(k):
        return pltpu.make_async_remote_copy(
            src_ref=sendm.at[k],
            dst_ref=recvm.at[k],
            send_sem=fm_send,
            recv_sem=fm_recv.at[lax.div(k, PER)],
            device_id=(peer_of(h, k, 1), me),
            device_id_type=MESH,
        )

    for c in range(CAP):
        r = idx_ref[c]
        recvq[0, pl.ds(c * CAND, CAND), :] = q_v[r]
        recvm[0, pl.ds(c, 1), :] = mrow_ref[r]

    def forward(k, carry):
        for c in range(CAP):
            r = idx_ref[k * CAP + c]
            sendq[k, pl.ds(c * CAND, CAND), :] = q_v[r]
            sendm[k, pl.ds(c, 1), :] = mrow_ref[r]
        fm_copy(k).start()
        fq_copy(k).start()
        return carry

    lax.fori_loop(1, NH, forward, 0)

    loads[2].wait()

    def w_copy(d):
        return pltpu.make_async_remote_copy(
            src_ref=wg_v.at[me],
            dst_ref=wg_v.at[me],
            send_sem=w_send.at[d - 1],
            recv_sem=w_recv.at[d - 1],
            device_id=(h, lax.rem(me + d, NX)),
            device_id_type=MESH,
        )

    def g_copy(d):
        return pltpu.make_async_remote_copy(
            src_ref=gain_ref,
            dst_ref=gains.at[me],
            send_sem=g_send.at[d - 1],
            recv_sem=g_recv.at[d - 1],
            device_id=(h, lax.rem(me + d, NX)),
            device_id_type=MESH,
        )

    for d in (2, 1, 3):
        g_copy(d).start()
        w_copy(d).start()
    gains[me] = gain_ref[...]

    def one_hot(t, carry):
        rows = pl.ds(pl.multiple_of(t * 128, 128), 128)
        i = lax.broadcasted_iota(jnp.int32, (128, 512), 0) + t * 128
        col = lax.broadcasted_iota(jnp.int32, (128, 512), 1)
        j, src, head = i >> 7, (i >> 4) & 7, (i >> 3) & 1
        slot, c = (i >> 2) & 1, i & 3
        want = head * 256 + src * 32 + slot * 16 + j * 4 + c
        perm[rows, :] = jnp.where(col == want, 1.0, 0.0).astype(BF16)
        return carry

    lax.fori_loop(0, 4, one_hot, 0)

    def placing(t, carry):
        rows = pl.ds(pl.multiple_of(t * 64, 64), 64)
        want = tgt_ref[rows, :]
        col = lax.broadcasted_iota(jnp.int32, (64, 1024), 1)
        for head in range(2):
            place[head, rows, :] = jnp.where(col == want + head * 8, 1.0, 0.0).astype(BF16)
        i = lax.broadcasted_iota(jnp.int32, (64, 1024), 0) + t * 64
        mine = (i >> 2) * 16 + me * SUB + (i & 3)
        pick = jnp.where(col == mine, 1.0, 0.0).astype(BF16)
        for b in range(NX):
            csub[b, rows, :] = jnp.dot(
                pick, cand_v[:, b * 256 : (b + 1) * 256], preferred_element_type=F32
            ).astype(BF16)
        return carry

    lax.fori_loop(0, 4, placing, 0)

    loads[3].wait()
    loads[4].wait()

    def x_copy(i, d):
        there = lax.rem(me + d, NX)
        return pltpu.make_async_remote_copy(
            src_ref=xs.at[i, there],
            dst_ref=xr.at[i, :, me],
            send_sem=x_send.at[d - 1],
            recv_sem=x_recv.at[i, d - 1],
            device_id=(h, there),
            device_id_type=MESH,
        )

    def a_copy(i, s):
        k = i * PER + s
        return pltpu.make_async_remote_copy(
            src_ref=xr.at[i, s],
            dst_ref=ans.at[k],
            send_sem=a_send,
            recv_sem=a_recv.at[i],
            device_id=(peer_of(h, k, -1), me),
            device_id_type=MESH,
        )

    def give_back(i):
        for d in range(1, NX):
            x_copy(i, d).wait_recv()

        def one(s, carry):
            a_copy(i, s).start()
            return carry

        @pl.when(i == 0)
        def _():
            ans[0] = xr[0, 0]
            lax.fori_loop(1, PER, one, 0)

        @pl.when(i > 0)
        def _():
            lax.fori_loop(0, PER, one, 0)

    def wait_chunk(buf, sem, i):
        @pl.when(i == 0)
        def _():
            part = buf.at[pl.ds(1, PER - 1)]
            pltpu.make_async_copy(part, part, sem.at[0]).wait()

        @pl.when(i > 0)
        def _():
            part = buf.at[pl.ds(i * PER, PER)]
            pltpu.make_async_copy(part, part, sem.at[i]).wait()

    half_scale = 0.5 * DH ** (-0.5)

    def attend(i, carry):
        wait_chunk(recvm, fm_recv, i)
        wait_chunk(recvq, fq_recv, i)
        for s in range(PER):
            for c in range(CAP):
                mexp[pl.ds((s * CAP + c) * CAND, CAND), :] = jnp.broadcast_to(
                    recvm[i * PER + s, pl.ds(c, 1), :], (CAND, 128)
                )
        q = recvq[pl.ds(i * PER, PER)].reshape(ROWS, 2 * DH)
        done = []
        for head in range(2):
            lanes = slice(head * DH, (head + 1) * DH)
            qh = q[:, lanes]
            total = None
            for u in range(2):
                for g in range(WIN // GRP):
                    first = u * HBLK + jnp.maximum(hb_ref[u] - WIN, 0) + g * GRP
                    keys = k_v[pl.ds(first, GRP), :, lanes].reshape(GRP * 128, DH)
                    vals = v_v[pl.ds(first, GRP), :, lanes].reshape(GRP * 128, DH)
                    s = lax.dot_general(
                        qh, keys, (((1,), (1,)), ((), ())), preferred_element_type=F32
                    )
                    parts = []
                    for b in range(GRP):
                        lane = u * WIN + g * GRP + b
                        v = s[:, b * 128 : (b + 1) * 128] * half_scale
                        w = (v + v * jnp.tanh(v)) * mexp[:, lane : lane + 1]
                        parts.append(w.astype(BF16))
                    w = jnp.concatenate(parts, axis=1)
                    r = jnp.dot(w, vals, preferred_element_type=F32)
                    total = r if total is None else total + r
            done.append(total.astype(BF16))
        stacked = jnp.concatenate(done, axis=0)
        moved = jnp.dot(perm[...], stacked, preferred_element_type=F32).astype(BF16)
        xs[i] = moved.reshape(NX, PER, CAND, DH)
        for d in (2, 1, 3):
            x_copy(i, d).start()
        xr[i, :, me] = xs[i, me]

        @pl.when(i > 0)
        def _():
            give_back(i - 1)

        return carry

    lax.fori_loop(0, CHUNKS, attend, 0)
    give_back(jnp.int32(CHUNKS - 1))

    for d in range(1, NX):
        w_copy(d).wait_recv()
        g_copy(d).wait_recv()

    def gate(b, carry):
        acc = jnp.zeros((256, 256), F32)
        for c in range(NX):
            acc += jnp.dot(
                csub[c], wg_v[b, c * 256 : (c + 1) * 256, :], preferred_element_type=F32
            )
        gg[b] = silu(acc) * gains[b]
        return carry

    lax.fori_loop(0, NX, gate, 0)
    for load in loads[5:]:
        load.wait()

    lax.fori_loop(0, CHUNKS, lambda i, c: (wait_chunk(ans, a_recv, i), c)[1], 0)

    for pair in range(2):
        rows = jnp.concatenate(
            [ans[:, 2 * pair + t].reshape(NH * CAND, DH) for t in range(2)], axis=1
        )
        for head in range(2):
            r = jnp.dot(place[head], rows, preferred_element_type=F32)
            for t in range(2):
                lo = ((2 * pair + t) * 2 + head) * DH
                att[:, lo : lo + DH] = r[:, t * DH : (t + 1) * DH]
    full = att[...]
    mean = jnp.sum(full, axis=-1, keepdims=True) * (1.0 / 1024)
    var = jnp.sum(full * full, axis=-1, keepdims=True) * (1.0 / 1024) - mean * mean
    rstd = 1.0 / jnp.sqrt(var + 1e-5)
    gated = [
        ((att[:, b * 256 : (b + 1) * 256] - mean) * rstd * gg[b]).astype(BF16)
        for b in range(NX)
    ]

    def o_copy(d):
        there = lax.rem(me + d, NX)
        return pltpu.make_async_remote_copy(
            src_ref=outs.at[there],
            dst_ref=out_ref.at[me],
            send_sem=o_send.at[d - 1],
            recv_sem=o_recv.at[d - 1],
            device_id=(h, there),
            device_id_type=MESH,
        )

    for d in (2, 1, 3, 0):
        there = lax.rem(me + d, NX)
        acc = csub[there].astype(F32)
        for b in range(NX):
            acc += jnp.dot(
                gated[b],
                wo_v[there, b * 256 : (b + 1) * 256, :],
                preferred_element_type=F32,
            )
        outs[there] = acc.astype(BF16)
        if d:
            o_copy(d).start()
    own = pltpu.make_async_copy(outs.at[me], out_ref.at[me], o_own)
    own.start()

    part = sendq.at[pl.ds(1, NH - 1)]
    pltpu.make_async_copy(part, part, fq_send).wait()
    part = sendm.at[pl.ds(1, NH - 1)]
    pltpu.make_async_copy(part, part, fm_send).wait()
    part = ans.at[pl.ds(1, NH - 1)]
    pltpu.make_async_copy(part, part, a_send).wait()
    for d in range(1, NX):
        part = xs.at[:, 0]
        pltpu.make_async_copy(part, part, x_send.at[d - 1]).wait()
        w_copy(d).wait_send()
        g_copy(d).wait_send()
    own.wait()
    for d in range(1, NX):
        o_copy(d).wait()


def on_device(
    candidates,
    w_gate,
    w_query,
    w_out,
    gain,
    key_cache,
    value_cache,
    hist_blocks,
    request_owner,
    request_slot,
    block_offsets,
):
    h = lax.axis_index("hist")
    owners = request_owner[:, 0]
    order = jnp.arange(REQ, dtype=jnp.int32)
    same_owner = owners[None, :] == owners[:, None]
    earlier = order[None, :] < order[:, None]
    rank = jnp.sum(jnp.where(same_owner & earlier, 1, 0), axis=1).astype(jnp.int32)
    dz = (owners // (NY * NC) - h // (NY * NC)) % NZ
    dy = (owners // NC % NY - h // NC % NY) % NY
    dc = (owners % NC + h % NC) % NC
    step = (dy * NC + dc - dz) % PER * PER + dz
    place = step * CAP + rank
    slots = jnp.arange(NH * CAP, dtype=jnp.int32)
    idx = jnp.sum(jnp.where(slots[:, None] == place[None, :], order[None, :], 0), axis=1)
    lane = request_slot[:, None] * WIN + WIN - 1 - block_offsets
    mrow = jnp.sum(
        jnp.where(lane[:, :, None] == jnp.arange(128, dtype=jnp.int32), 1.0, 0.0), axis=1
    ).reshape(REQ, 1, 128)
    tgt = (step * 16 + rank * SUB)[:, None] + jnp.arange(SUB, dtype=jnp.int32)
    tgt = tgt.reshape(REQ * SUB, 1)

    vmem = pl.BlockSpec(memory_space=pltpu.VMEM)
    smem = pl.BlockSpec(memory_space=pltpu.SMEM)
    anyw = pl.BlockSpec(memory_space=pl.ANY)
    dma = pltpu.SemaphoreType.DMA
    out = pl.pallas_call(
        kernel,
        out_shape=jax.ShapeDtypeStruct((NX, REQ * SUB, 256), BF16),
        in_specs=[smem, smem, vmem, vmem, vmem] + [anyw] * 6,
        out_specs=anyw,
        scratch_shapes=[
            pltpu.VMEM((1024, 1024), BF16),
            pltpu.VMEM((1024, 256), BF16),
            pltpu.VMEM((NX, 1024, 256), BF16),
            pltpu.VMEM((NX, 1024, 256), BF16),
            pltpu.VMEM((2 * HBLK, 128, 256), BF16),
            pltpu.VMEM((2 * HBLK, 128, 256), BF16),
            pltpu.VMEM((REQ, CAND, 256), BF16),
            pltpu.VMEM((NH, CAP * CAND, 256), BF16),
            pltpu.VMEM((NH, CAP, 128), F32),
            pltpu.VMEM((NH, CAP * CAND, 256), BF16),
            pltpu.VMEM((NH, CAP, 128), F32),
            pltpu.VMEM((ROWS, 128), F32),
            pltpu.VMEM((CHUNKS, NX, PER, CAND, DH), BF16),
            pltpu.VMEM((CHUNKS, PER, NX, CAND, DH), BF16),
            pltpu.VMEM((NH, NX, CAND, DH), BF16),
            pltpu.VMEM((512, 512), BF16),
            pltpu.VMEM((2, 256, 1024), BF16),
            pltpu.VMEM((NX, 256, 256), BF16),
            pltpu.VMEM((NX, 256, 256), F32),
            pltpu.VMEM((NX, 1, 256), F32),
            pltpu.VMEM((256, 1024), F32),
            pltpu.VMEM((NX, 256, 256), BF16),
            dma((9,)),
            dma,
            dma,
            dma((CHUNKS,)),
            dma((CHUNKS,)),
            dma((3,)),
            dma((3,)),
            dma((3,)),
            dma((3,)),
            dma((3,)),
            dma((CHUNKS, 3)),
            dma,
            dma((CHUNKS,)),
            dma((3,)),
            dma((3,)),
            dma,
        ],
        compiler_params=pltpu.CompilerParams(
            collective_id=0, has_side_effects=True, vmem_limit_bytes=56 * 1024 * 1024
        ),
        name="attend_remote",
    )(
        idx,
        hist_blocks,
        mrow,
        tgt,
        gain.reshape(1, 256),
        candidates,
        w_query,
        w_gate,
        w_out,
        key_cache.reshape(2 * HBLK, 128, 256),
        value_cache.reshape(2 * HBLK, 128, 256),
    )
    return out.reshape(NX, REQ, SUB, 256).transpose(1, 0, 2, 3).reshape(REQ * CAND, 256)


def solution(mesh):
    in_specs = (
        P("hist", None),
        P(None, "mp"),
        P(None, "mp"),
        P(),
        P("mp"),
        P("hist", None, "mp"),
        P("hist", None, "mp"),
        P("hist"),
        P("hist", None),
        P("hist"),
        P("hist", None),
    )
    return jax.shard_map(
        on_device, mesh=mesh, in_specs=in_specs, out_specs=P("hist", "mp"), check_vma=False
    )
```

time: 260 us -> 92.1 us (0.35)
  waiting for transfers between devices: 88.6 us -> 0 us
  Pallas kernels: 0 us -> 83.6 us
  matrix products: 54.9 us -> 0 us
  local copies, waits for them, and re-layouts: 49.9 us -> 3.02 us
  starting transfers between devices: 30 us -> 0 us
  between operations: 14.9 us -> 0.03 us
  blocking collectives: 8.59 us -> 0 us
  other arithmetic: 11.7 us -> 5.18 us
    pallas_call x0 -> x1, Pallas kernels: none -> 83.6 us  [on_device(): pl.pallas_call(kernel, out_shape=jax.ShapeDtypeStruct((NX, REQ * SUB, 256...]
    dot_general x28 -> x0, matrix products: 54.9 us -> none  [the longest x8 28.4 us: attend_group(): jnp.einsum('gchd,khd->ghck', query_group, window_keys, preferred_element_...]
    reduce_scatter x1 -> x0, waiting for transfers between devices: 46.5 us -> none  [on_device(): mine = lax.psum_scatter(partial_out, 'mp', scatter_dimension=1, tiled=True)]
    all_to_all x3 -> x0, waiting for transfers between devices: 42.1 us -> none  [the longest x1 27.9 us: on_device(): lax.all_to_all(outcome, 'hist', split_axis=0, concat_axis=0, tiled=True)]
    all_to_all x3 -> x0, starting transfers between devices: 29.9 us -> none  [the longest x1 13.2 us: on_device(): lax.all_to_all(send_info, 'hist', split_axis=0, concat_axis=0, tiled=True)]
    dynamic_slice x10 -> x0, local copies, waits for them, and re-layouts: 11.8 us -> none  [the longest x8 7.96 us: on_device(): outcome = lax.map(attend_group, (grouped_query, grouped_multiple))]
    unnamed x12 -> x0, local copies, waits for them, and re-layouts: 9.98 us -> none
    psum x1 -> x0, blocking collectives: 8.59 us -> none  [on_device(): lax.psum((jnp.sum(widened, axis=-1), jnp.sum(widened * widened, axis=-1))...]
  transfers between devices with their start and end apart: 4 -> 0, of which waited for: 3 -> 0; matrix products, arithmetic and copies ran while one was open for 14% -> 0% of each run, Pallas kernels for 0% -> 0%
where the time goes in v1:
time: 92.1 us; the launch traced here: 91.8 us
  Pallas kernels  83.6 us (91%)
  other arithmetic  5.18 us (6%)
  local copies, waits for them, and re-layouts  3.02 us (3%)
    pallas_call x1, Pallas kernels, on_device(): pl.pallas_call(kernel, out_shape=jax.ShapeDtypeStruct((NX, REQ * SUB, 256...  83.6 us
    reshape x2, local copies, waits for them, and re-layouts, on_device(): out.reshape(NX, REQ, SUB, 256).transpose(1, 0, 2, 3)  2.08 us

profile of v1, /device:TPU:1, one launch (start us, length us, event | category | flops | bytes accessed | tf_op | source)
XLA Modules:
  0.0 91.8 jit_solution(9630116198405327615)
XLA Ops:
  0.0 0.9 select_reduce_fusion.2
  0.9 0.7 fusion.25
  1.6 0.7 multiply_add_fusion.1
  2.3 0.7 select_reduce_fusion.1.idx_ref
  3.0 0.7 multiply_add_fusion
  3.6 0.7 broadcast_subtract_fusion
  4.3 0.8 select_reduce_fusion
  5.1 0.1 iota_add_fusion
  5.2 0.8 add.195.tgt_ref
  5.9 83.6 %attend_remote.1 = bf16[4,256,256]{2,1,0:T(8,128)(2,1)} custom-call(s32[128]{0:T(128)} %select_reduce_fusion.1.idx_ref, s32[2]{0:T(128)} %hb_ref.1, f32[64,1,128]{2,1,0:T(1,128)} %bitcast.16, s32[256,1]{1,0:T(8,128)} %add.195.tgt_ref, f32[1,256]{1,0:T(1,128)} %bitcast.18, bf16[1024,1024]{1,0:T(8,128)(2,1)} %cand_hbm.1, bf16[1024,256]{1,0:T(8,128)(2,1)} %wq_hbm.1, ...), custom_call_target="tpu_custom_call" | custom-call | tf_op jit(solution)/shard_map/attend_remote/pallas_call | solution.py:457
  89.6 1.2 %reshape.185 = bf16[4,64,4,256]{3,2,1,0:T(4,128)(2,1)S(1)} reshape(bf16[4,256,256]{2,1,0:T(8,128)(2,1)} %attend_remote.1) | data formatting | bytes 1048576 | tf_op jit(solution)/shard_map/reshape | solution.py:519
  90.7 0.2 copy.18
  90.9 0.9 reshape.186

commit v2 on v1

v2 whole, which is shorter than its diff:
```python
import jax
import jax.numpy as jnp
from jax import lax
from jax.experimental import pallas as pl
from jax.experimental.pallas import tpu as pltpu
from jax.sharding import PartitionSpec as P

MESH = pl.DeviceIdType.MESH
F32 = jnp.float32
BF16 = jnp.bfloat16

NZ, NY, NC = 8, 4, 2
NH = NZ * NY * NC
CHUNKS, PER = 8, 8
NX = 4
CAP = 2
CAND = 16
REQ = 64
DH = 128
WIN = 12
HBLK = 24
SUB = CAND // NX
ROWS = PER * CAP * CAND
GRP = 4
UPFRONT = 8


def peer_of(h, low, dz, sign):
    z, y, c = h >> 3, (h >> 1) & 3, h & 1
    z = (z + sign * dz) & (NZ - 1)
    y = (y + sign * (low >> 1)) & (NY - 1)
    return z * (NY * NC) + y * NC + (c ^ (low & 1))


def silu(v):
    half = v * 0.5
    return half + half * jnp.tanh(half)


def kernel(
    hb_ref,
    own_ref,
    slot_ref,
    off_ref,
    gain_ref,
    cand_hbm,
    wq_hbm,
    wg_hbm,
    wo_hbm,
    k_hbm,
    v_hbm,
    out_ref,
    cand_v,
    wq_v,
    wg_v,
    wo_v,
    k_v,
    v_v,
    q_v,
    tcol,
    mall,
    sendq,
    sendm,
    recvq,
    recvm,
    mexp,
    xs,
    xr,
    ans,
    perm,
    place,
    csub,
    r4,
    gs,
    gr,
    att,
    outs,
    kt,
    load_sem,
    fq_send,
    fm_send,
    fq_recv,
    fm_recv,
    g_send,
    g_recv,
    x_send,
    x_recv,
    a_send,
    a_recv,
    o_send,
    o_recv,
    plane_sem,
    own_sem,
):
    h = lax.axis_index("hist")
    me = lax.axis_index("mp")

    barrier = pltpu.get_barrier_semaphore()

    def greet(sem, low, dz):
        pl.semaphore_signal(
            sem, inc=1, device_id=(peer_of(h, low, dz, 1), me), device_id_type=MESH
        )

    for d in range(1, PER):
        greet(barrier, 0, d)
    for d in range(1, NX):
        pl.semaphore_signal(
            barrier, inc=1, device_id=(h, lax.rem(me + d, NX)), device_id_type=MESH
        )
    for d in range(1, CHUNKS):
        greet(barrier, d, 0)

    loads = [
        pltpu.make_async_copy(cand_hbm, cand_v, load_sem.at[0]),
        pltpu.make_async_copy(wq_hbm, wq_v, load_sem.at[1]),
        pltpu.make_async_copy(wg_hbm, wg_v, load_sem.at[2]),
        pltpu.make_async_copy(k_hbm, k_v, load_sem.at[3]),
        pltpu.make_async_copy(v_hbm, v_v, load_sem.at[4]),
    ] + [
        pltpu.make_async_copy(
            wo_hbm.at[:, pl.ds(b * 256, 256)], wo_v.at[b], load_sem.at[5 + b]
        )
        for b in range(NX)
    ]
    for load in loads[:2]:
        load.start()

    def same_lanes(row, count):
        return jnp.broadcast_to(row, (count, REQ))

    def lanes_dot(a, b):
        return lax.dot_general(a, b, (((1,), (1,)), ((), ())), preferred_element_type=F32)

    def iota(shape, axis):
        return lax.broadcasted_iota(jnp.int32, shape, axis)

    def flag(hit):
        return jnp.where(hit, 1.0, 0.0)

    own = own_ref[...]
    own_f = own.astype(F32)
    eye = flag(iota((REQ, REQ), 0) == iota((REQ, REQ), 1)).astype(BF16)
    own_col = lanes_dot(eye, same_lanes(own_f, REQ).astype(BF16))
    twin = (own_col == same_lanes(own_f, REQ)) & (iota((REQ, REQ), 0) < iota((REQ, REQ), 1))
    rank = jnp.sum(flag(twin), axis=0, keepdims=True)
    low_own, low_h = own & (NY * NC - 1), lax.rem(h, NY * NC)
    dz = ((own >> 3) - lax.div(h, NY * NC) + NZ) & (NZ - 1)
    dy = ((low_own >> 1) - lax.div(low_h, NC) + NY) & (NY - 1)
    dc = (low_own + lax.rem(low_h, NC)) & (NC - 1)
    step = (dy * NC + dc) * PER + dz
    slot = (step * CAP).astype(F32) + rank
    slot_bf = same_lanes(slot, 128).astype(BF16)
    spread = flag(iota((REQ, 1024), 1) >> 4 == iota((REQ, 1024), 0)).astype(BF16)
    tcol[...] = jnp.dot(
        slot_bf[:8], spread, preferred_element_type=F32
    ) * CAND + (iota((8, 1024), 1) & (CAND - 1)).astype(F32)
    lane = slot_ref[...] * WIN + (WIN - 1)
    counts = jnp.zeros((32, REQ), F32)
    for j in range(WIN):
        counts += flag(same_lanes(lane - off_ref[pl.ds(j, 1), :], 32) == iota((32, REQ), 0))
    blank = jnp.zeros((32, REQ), F32)
    both = jnp.zeros((NH, 128), F32)
    for c in range(CAP):
        parts = [blank] * (2 * c) + [counts] + [blank] * (3 - 2 * c)
        mine = (iota((NH, REQ), 0) * CAP + c).astype(F32)
        held = flag(same_lanes(slot, NH) == mine).astype(BF16)
        both += lanes_dot(held, jnp.concatenate(parts, axis=0).astype(BF16))
    mall[...] = both

    loads[0].wait()
    loads[1].wait()
    for load in loads[2:]:
        load.start()

    def project(t, carry):
        rows = pl.ds(pl.multiple_of(t * 256, 256), 256)
        acc = jnp.dot(cand_v[rows, :], wq_v[...], preferred_element_type=F32)
        q_v[rows, :] = silu(acc).astype(BF16)
        return carry

    lax.fori_loop(0, 4, project, 0)

    pl.semaphore_wait(barrier, PER - 1 + CHUNKS - 1 + NX - 1)
    for d in range(1, CHUNKS):
        greet(plane_sem, d, 0)

    def fq_copy(i, dz):
        k = i * PER + dz
        return pltpu.make_async_remote_copy(
            src_ref=sendq.at[k],
            dst_ref=recvq.at[k],
            send_sem=fq_send,
            recv_sem=fq_recv.at[i],
            device_id=(peer_of(h, i, dz, 1), me),
            device_id_type=MESH,
        )

    def fm_copy(i, dz):
        k = i * PER + dz
        return pltpu.make_async_remote_copy(
            src_ref=sendm.at[k],
            dst_ref=recvm.at[k],
            send_sem=fm_send,
            recv_sem=fm_recv.at[i],
            device_id=(peer_of(h, i, dz, 1), me),
            device_id_type=MESH,
        )

    def forward(i, carry):
        row = (iota((ROWS, 1024), 0) + i * ROWS).astype(F32)
        pick = flag(row == jnp.broadcast_to(tcol[pl.ds(0, 1), :], (ROWS, 1024))).astype(BF16)
        got = jnp.dot(pick, q_v[...], preferred_element_type=F32).astype(BF16)
        sendq[pl.ds(i * PER, PER)] = got.reshape(PER, CAP * CAND, 2 * DH)

        def one(dz):
            k = i * PER + dz
            sendm[k] = mall[pl.ds(k, 1), :]
            fm_copy(i, dz).start()
            fq_copy(i, dz).start()

        @pl.when(i == 0)
        def _():
            recvq[0] = sendq[0]
            recvm[0] = mall[pl.ds(0, 1), :]

        @pl.when(i == 1)
        def _():
            pl.semaphore_wait(plane_sem, CHUNKS - 1)

        @pl.when(i > 0)
        def _():
            one(0)

        for dz in range(1, PER):
            one(dz)

        return carry

    lax.fori_loop(0, UPFRONT, forward, 0)

    def g_copy(d):
        there = lax.rem(me + d, NX)
        return pltpu.make_async_remote_copy(
            src_ref=gs.at[there],
            dst_ref=gr.at[me],
            send_sem=g_send.at[d - 1],
            recv_sem=g_recv.at[d - 1],
            device_id=(h, there),
            device_id_type=MESH,
        )

    i, col = iota((256, 256), 0), iota((256, 256), 1)
    r4[...] = flag(col == ((i >> 2) & 15) * 16 + (i >> 6) * 4 + (i & 3)).astype(BF16)

    loads[2].wait()

    def gate(t, carry):
        rows = pl.ds(pl.multiple_of(t * 256, 256), 256)
        part = pl.ds(pl.multiple_of(t * 64, 64), 64)
        acc = jnp.dot(cand_v[rows, :], wg_v[...], preferred_element_type=F32)
        g = (silu(acc) * gain_ref[...]).astype(BF16)
        moved = jnp.dot(r4[...], g, preferred_element_type=F32).astype(BF16)
        gs[:, part, :] = moved.reshape(NX, 64, 256)
        mine = r4[pl.ds(pl.multiple_of(me * 64, 64), 64), :]
        for b in range(NX):
            csub[b, part, :] = jnp.dot(
                mine, cand_v[rows, b * 256 : (b + 1) * 256], preferred_element_type=F32
            ).astype(BF16)
        return carry

    lax.fori_loop(0, 4, gate, 0)
    gr[me] = gs[me]

    def one_hot(t, carry):
        rows = pl.ds(pl.multiple_of(t * 128, 128), 128)
        i = lax.broadcasted_iota(jnp.int32, (128, 512), 0) + t * 128
        col = lax.broadcasted_iota(jnp.int32, (128, 512), 1)
        j, src, head = i >> 7, (i >> 4) & 7, (i >> 3) & 1
        slot, c = (i >> 2) & 1, i & 3
        want = head * 256 + src * 32 + slot * 16 + j * 4 + c
        perm[rows, :] = jnp.where(col == want, 1.0, 0.0).astype(BF16)
        return carry

    lax.fori_loop(0, 4, one_hot, 0)

    i = iota((256, REQ), 0)
    spread = flag(i >> 2 == iota((256, REQ), 1)).astype(BF16)
    want = lanes_dot(spread, slot_bf)
    c = iota((256, 128), 0) & 3
    for t in range(8):
        col = iota((256, 128), 1) + t * 128
        for head in range(2):
            sits = ((col >> 4) * 2 + ((col >> 2) & 1)).astype(F32)
            hit = (sits == want) & ((col & 3) == c) & (((col >> 3) & 1) == head)
            place[head, :, t * 128 : (t + 1) * 128] = flag(hit).astype(BF16)

    loads[3].wait()
    for b in range(WIN):
        for u in range(2):
            first = u * HBLK + jnp.maximum(hb_ref[u] - WIN, 0) + b
            for head in range(2):
                kt[u * 2 + head, :, b * 128 : (b + 1) * 128] = k_v[
                    first, :, head * DH : (head + 1) * DH
                ].T
    loads[4].wait()

    def x_copy(i, d):
        there = lax.rem(me + d, NX)
        return pltpu.make_async_remote_copy(
            src_ref=xs.at[i, there],
            dst_ref=xr.at[i, :, me],
            send_sem=x_send.at[d - 1],
            recv_sem=x_recv.at[i, d - 1],
            device_id=(h, there),
            device_id_type=MESH,
        )

    def a_copy(i, s):
        k = i * PER + s
        return pltpu.make_async_remote_copy(
            src_ref=xr.at[i, s],
            dst_ref=ans.at[k],
            send_sem=a_send,
            recv_sem=a_recv.at[i],
            device_id=(peer_of(h, i, s, -1), me),
            device_id_type=MESH,
        )

    def give_back(i):
        for d in range(1, NX):
            x_copy(i, d).wait_recv()

        @pl.when(i == 0)
        def _():
            ans[0] = xr[0, 0]

        @pl.when(i > 0)
        def _():
            a_copy(i, 0).start()

        for s in range(1, PER):
            a_copy(i, s).start()

    def wait_chunk(buf, sem, i):
        @pl.when(i == 0)
        def _():
            part = buf.at[pl.ds(1, PER - 1)]
            pltpu.make_async_copy(part, part, sem.at[0]).wait()

        @pl.when(i > 0)
        def _():
            part = buf.at[pl.ds(i * PER, PER)]
            pltpu.make_async_copy(part, part, sem.at[i]).wait()

    half_scale = 0.5 * DH ** (-0.5)

    def attend(i, carry):
        wait_chunk(recvm, fm_recv, i)
        wait_chunk(recvq, fq_recv, i)
        for s in range(PER):
            for c in range(CAP):
                mexp[pl.ds((s * CAP + c) * CAND, CAND), :] = jnp.broadcast_to(
                    recvm[i * PER + s, :, c * 64 : c * 64 + 64], (CAND, 64)
                )
        q = recvq[pl.ds(i * PER, PER)].reshape(ROWS, 2 * DH)
        done = []
        for head in range(2):
            lanes = slice(head * DH, (head + 1) * DH)
            qh = q[:, lanes]
            total = None
            for u in range(2):
                for g in range(WIN // GRP):
                    first = u * HBLK + jnp.maximum(hb_ref[u] - WIN, 0) + g * GRP
                    vals = v_v[pl.ds(first, GRP), :, lanes].reshape(GRP * 128, DH)
                    s = jnp.dot(
                        qh,
                        kt[u * 2 + head, :, g * GRP * 128 : (g + 1) * GRP * 128],
                        preferred_element_type=F32,
                    )
                    parts = []
                    for b in range(GRP):
                        lane = u * WIN + g * GRP + b
                        v = s[:, b * 128 : (b + 1) * 128] * half_scale
                        w = (v + v * jnp.tanh(v)) * mexp[:, lane : lane + 1]
                        parts.append(w.astype(BF16))
                    w = jnp.concatenate(parts, axis=1)
                    r = jnp.dot(w, vals, preferred_element_type=F32)
                    total = r if total is None else total + r
            done.append(total.astype(BF16))
        stacked = jnp.concatenate(done, axis=0)
        moved = jnp.dot(perm[...], stacked, preferred_element_type=F32).astype(BF16)
        xs[i] = moved.reshape(NX, PER, CAND, DH)
        for d in (2, 1, 3):
            x_copy(i, d).start()
        xr[i, :, me] = xs[i, me]
        for at, d in ((2, 2), (3, 1), (4, 3)):

            @pl.when(i == at)
            def _(d=d):
                g_copy(d).start()


        @pl.when(i > 0)
        def _():
            give_back(i - 1)

        return carry

    lax.fori_loop(0, CHUNKS, attend, 0)
    give_back(jnp.int32(CHUNKS - 1))

    for d in range(1, NX):
        g_copy(d).wait_recv()
    for load in loads[5:]:
        load.wait()

    for p in range(CHUNKS // 2):
        wait_chunk(ans, a_recv, jnp.int32(2 * p))
        wait_chunk(ans, a_recv, jnp.int32(2 * p + 1))
        got = ans[pl.ds(p * 2 * PER, 2 * PER)]
        rows = jnp.concatenate(
            [got[:, x].reshape(2 * PER * CAND, DH) for x in range(NX)], axis=1
        )
        for head in range(2):
            r = jnp.dot(
                place[head, :, p * 256 : (p + 1) * 256], rows, preferred_element_type=F32
            )
            for x in range(NX):
                lo = (x * 2 + head) * DH
                part = r[:, x * DH : (x + 1) * DH]
                if p:
                    part = part + att[:, lo : lo + DH]
                att[:, lo : lo + DH] = part

    def o_copy(t, d):
        there = lax.rem(me + d, NX)
        part = pl.ds(t * 128, 128)
        return pltpu.make_async_remote_copy(
            src_ref=outs.at[there, part],
            dst_ref=out_ref.at[me, part],
            send_sem=o_send.at[t, d - 1],
            recv_sem=o_recv.at[t, d - 1],
            device_id=(h, there),
            device_id_type=MESH,
        )

    def o_own(t):
        part = pl.ds(t * 128, 128)
        return pltpu.make_async_copy(outs.at[me, part], out_ref.at[me, part], own_sem.at[t])

    for t in range(2):
        part = pl.ds(t * 128, 128)
        full = att[part, :]
        mean = jnp.sum(full, axis=-1, keepdims=True) * (1.0 / 1024)
        var = jnp.sum(full * full, axis=-1, keepdims=True) * (1.0 / 1024) - mean * mean
        rstd = 1.0 / jnp.sqrt(var + 1e-5)
        gated = jnp.concatenate(
            [
                ((att[part, b * 256 : (b + 1) * 256] - mean) * rstd * gr[b, part].astype(F32))
                .astype(BF16)
                for b in range(NX)
            ],
            axis=1,
        )
        for d in (2, 1, 3, 0):
            there = lax.rem(me + d, NX)
            acc = csub[there, part].astype(F32) + jnp.dot(
                gated, wo_v[there], preferred_element_type=F32
            )
            if d:
                outs[there, part] = acc.astype(BF16)
                o_copy(t, d).start()
            else:
                outs[there, part] = acc.astype(BF16)
                o_own(t).start()

    for t in range(2):
        o_own(t).wait()
        for d in range(1, NX):
            o_copy(t, d).wait_recv()

    part = sendq.at[pl.ds(1, NH - 1)]
    pltpu.make_async_copy(part, part, fq_send).wait()
    part = sendm.at[pl.ds(1, NH - 1)]
    pltpu.make_async_copy(part, part, fm_send).wait()
    part = ans.at[pl.ds(1, NH - 1)]
    pltpu.make_async_copy(part, part, a_send).wait()
    for d in range(1, NX):
        part = xs.at[:, 0]
        pltpu.make_async_copy(part, part, x_send.at[d - 1]).wait()
        g_copy(d).wait_send()
    for d in range(1, NX):
        o_copy(0, d).wait_send()
        o_copy(1, d).wait_send()


def on_device(
    candidates,
    w_gate,
    w_query,
    w_out,
    gain,
    key_cache,
    value_cache,
    hist_blocks,
    request_owner,
    request_slot,
    block_offsets,
):
    vmem = pl.BlockSpec(memory_space=pltpu.VMEM)
    smem = pl.BlockSpec(memory_space=pltpu.SMEM)
    anyw = pl.BlockSpec(memory_space=pl.ANY)
    dma = pltpu.SemaphoreType.DMA
    out = pl.pallas_call(
        kernel,
        out_shape=jax.ShapeDtypeStruct((NX, REQ * SUB, 256), BF16),
        in_specs=[smem, vmem, vmem, vmem, vmem] + [anyw] * 6,
        out_specs=anyw,
        scratch_shapes=[
            pltpu.VMEM((1024, 1024), BF16),
            pltpu.VMEM((1024, 256), BF16),
            pltpu.VMEM((1024, 256), BF16),
            pltpu.VMEM((NX, 1024, 256), BF16),
            pltpu.VMEM((2 * HBLK, 128, 256), BF16),
            pltpu.VMEM((2 * HBLK, 128, 256), BF16),
            pltpu.VMEM((1024, 256), BF16),
            pltpu.VMEM((8, 1024), F32),
            pltpu.VMEM((NH, 128), F32),
            pltpu.VMEM((NH, CAP * CAND, 256), BF16),
            pltpu.VMEM((NH, 1, 128), F32),
            pltpu.VMEM((NH, CAP * CAND, 256), BF16),
            pltpu.VMEM((NH, 1, 128), F32),
            pltpu.VMEM((ROWS, 64), F32),
            pltpu.VMEM((CHUNKS, NX, PER, CAND, DH), BF16),
            pltpu.VMEM((CHUNKS, PER, NX, CAND, DH), BF16),
            pltpu.VMEM((NH, NX, CAND, DH), BF16),
            pltpu.VMEM((512, 512), BF16),
            pltpu.VMEM((2, 256, 1024), BF16),
            pltpu.VMEM((NX, 256, 256), BF16),
            pltpu.VMEM((256, 256), BF16),
            pltpu.VMEM((NX, 256, 256), BF16),
            pltpu.VMEM((NX, 256, 256), BF16),
            pltpu.VMEM((256, 1024), F32),
            pltpu.VMEM((NX, 256, 256), BF16),
            pltpu.VMEM((4, DH, WIN * 128), BF16),
            dma((9,)),
            dma,
            dma,
            dma((CHUNKS,)),
            dma((CHUNKS,)),
            dma((3,)),
            dma((3,)),
            dma((3,)),
            dma((CHUNKS, 3)),
            dma,
            dma((CHUNKS,)),
            dma((2, 3)),
            dma((2, 3)),
            pltpu.SemaphoreType.REGULAR,
            dma((2,)),
        ],
        compiler_params=pltpu.CompilerParams(
            collective_id=0, has_side_effects=True, vmem_limit_bytes=56 * 1024 * 1024
        ),
        name="attend_remote",
    )(
        hist_blocks,
        request_owner.reshape(1, REQ),
        request_slot.reshape(1, REQ),
        block_offsets.T,
        gain.reshape(1, 256),
        candidates,
        w_query,
        w_gate,
        w_out,
        key_cache.reshape(2 * HBLK, 128, 256),
        value_cache.reshape(2 * HBLK, 128, 256),
    )
    return out.reshape(NX, REQ, SUB, 256).transpose(1, 0, 2, 3).reshape(REQ * CAND, 256)


def solution(mesh):
    in_specs = (
        P("hist", None),
        P(None, "mp"),
        P(None, "mp"),
        P(),
        P("mp"),
        P("hist", None, "mp"),
        P("hist", None, "mp"),
        P("hist"),
        P("hist", None),
        P("hist"),
        P("hist", None),
    )
    return jax.shard_map(
        on_device, mesh=mesh, in_specs=in_specs, out_specs=P("hist", "mp"), check_vma=False
    )
```

time: 92.1 us -> 73 us (0.79)
  Pallas kernels: 83.6 us -> 70.5 us
  other arithmetic: 5.18 us -> 0 us
    pallas_call x1, Pallas kernels: 83.6 us -> 70.5 us  [on_device(): pl.pallas_call(kernel, out_shape=jax.ShapeDtypeStruct((NX, REQ * SUB, 256...]
    reduce_sum x3 -> x0, other arithmetic: 2.35 us -> none  [the longest x1 0.91 us: on_device(): jnp.sum(jnp.where(same_owner & earlier, 1, 0), axis=1).astype(jnp.int32)]
    add x3 -> x0, other arithmetic: 1.47 us -> none  [the longest x2 0.78 us: on_device(): tgt = (step * 16 + rank * SUB)[:, None] + jnp.arange(SUB, dtype=jnp.int32)]
    sub x2 -> x0, other arithmetic: 1.36 us -> none  [on_device(): lane = request_slot[:, None] * WIN + WIN - 1 - block_offsets]
where the time goes in v2:
time: 73 us; the launch traced here: 72.8 us
  Pallas kernels  70.5 us (97%)
  local copies, waits for them, and re-layouts  2.27 us (3%)
    pallas_call x1, Pallas kernels, on_device(): pl.pallas_call(kernel, out_shape=jax.ShapeDtypeStruct((NX, REQ * SUB, 256...  70.5 us
    reshape x2, local copies, waits for them, and re-layouts, on_device(): out.reshape(NX, REQ, SUB, 256).transpose(1, 0, 2, 3)  2.08 us

profile of v2, /device:TPU:1, one launch (start us, length us, event | category | flops | bytes accessed | tf_op | source)
XLA Modules:
  0.0 72.8 jit_solution(8076191469988203323)
XLA Ops:
  0.0 70.5 %attend_remote.1 = bf16[4,256,256]{2,1,0:T(8,128)(2,1)} custom-call(s32[2]{0:T(128)} %hb_ref.1, s32[1,64]{1,0:T(1,128)} %bitcast.12, s32[1,64]{1,0:T(1,128)} %bitcast.13, s32[12,64]{1,0:T(8,128)} %bitcast.10, f32[1,256]{1,0:T(1,128)} %bitcast.11, bf16[1024,1024]{1,0:T(8,128)(2,1)} %cand_hbm.1, bf16[1024,256]{1,0:T(8,128)(2,1)} %wq_hbm.1, ...), custom_call_target="tpu_custom_call" | custom-call | tf_op jit(solution)/shard_map/attend_remote/pallas_call | solution.py:515
  70.5 1.2 %reshape.26 = bf16[4,64,4,256]{3,2,1,0:T(4,128)(2,1)S(1)} reshape(bf16[4,256,256]{2,1,0:T(8,128)(2,1)} %attend_remote.1) | data formatting | bytes 1048576 | tf_op jit(solution)/shard_map/reshape | solution.py:580
  71.7 0.2 copy.12
  71.9 0.9 %reshape.27 = bf16[1024,256]{1,0:T(8,128)(2,1)} reshape(bf16[64,4,4,256]{3,2,1,0:T(4,128)(2,1)S(1)} %copy.12) | data formatting | bytes 1048576 | tf_op jit(solution)/shard_map/reshape | solution.py:580

commit v3 on v2

--- a/solution.py
+++ b/solution.py
@@ -493,6 +493,18 @@
     for d in range(1, NX):
         o_copy(0, d).wait_send()
         o_copy(1, d).wait_send()
+
+
+def interleave(in_ref, out_ref):
+    i = lax.broadcasted_iota(jnp.int32, (256, 256), 0)
+    col = lax.broadcasted_iota(jnp.int32, (256, 256), 1)
+    put = jnp.where(i == ((col >> 2) & 15) * 16 + (col >> 6) * 4 + (col & 3), 1.0, 0.0)
+    put = put.astype(BF16)
+    for t in range(2):
+        rows = in_ref[:, t * 64 : (t + 1) * 64, :].reshape(256, 256)
+        out_ref[t * 256 : (t + 1) * 256, :] = jnp.dot(
+            put, rows, preferred_element_type=F32
+        ).astype(BF16)
 
 
 def on_device(
@@ -577,7 +589,14 @@
         key_cache.reshape(2 * HBLK, 128, 256),
         value_cache.reshape(2 * HBLK, 128, 256),
     )
-    return out.reshape(NX, REQ, SUB, 256).transpose(1, 0, 2, 3).reshape(REQ * CAND, 256)
+    return pl.pallas_call(
+        interleave,
+        out_shape=jax.ShapeDtypeStruct((REQ * CAND, 256), BF16),
+        grid=(2,),
+        in_specs=[pl.BlockSpec((NX, 128, 256), lambda t: (0, t, 0))],
+        out_specs=pl.BlockSpec((512, 256), lambda t: (t, 0)),
+        name="interleave_rows",
+    )(out)
 
 
 def solution(mesh):

time: 73 us -> 72.8 us (level)
  local copies, waits for them, and re-layouts: 2.27 us -> 0 us
  Pallas kernels: 70.5 us -> 72.7 us
    pallas_call x0 -> x1, Pallas kernels: none -> 2.15 us  [on_device(): pl.pallas_call(interleave, out_shape=jax.ShapeDtypeStruct((REQ * CAND, 25...]
    reshape x2 -> x0, local copies, waits for them, and re-layouts: 2.08 us -> none  [on_device(): out.reshape(NX, REQ, SUB, 256).transpose(1, 0, 2, 3)]
where the time goes in v3:
time: 72.8 us; the launch traced here: 72.7 us
  Pallas kernels  72.7 us (100%)
    pallas_call x1, Pallas kernels, on_device(): pl.pallas_call(kernel, out_shape=jax.ShapeDtypeStruct((NX, REQ * SUB, 256...  70.5 us
    pallas_call x1, Pallas kernels, on_device(): pl.pallas_call(interleave, out_shape=jax.ShapeDtypeStruct((REQ * CAND, 25...  2.15 us

profile of v3, /device:TPU:1, one launch (start us, length us, event | category | flops | bytes accessed | tf_op | source)
XLA Modules:
  0.0 72.7 jit_solution(6883782677290495571)
XLA Ops:
  0.0 70.5 %attend_remote.1.in_ref = bf16[4,256,256]{2,1,0:T(8,128)(2,1)} custom-call(s32[2]{0:T(128)} %hb_ref.1, s32[1,64]{1,0:T(1,128)} %bitcast.10, s32[1,64]{1,0:T(1,128)} %bitcast.11, s32[12,64]{1,0:T(8,128)} %bitcast.8, f32[1,256]{1,0:T(1,128)} %bitcast.9, bf16[1024,1024]{1,0:T(8,128)(2,1)} %cand_hbm.1, bf16[1024,256]{1,0:T(8,128)(2,1)} %wq_hbm.1, ...), custom_call_target="tpu_custom_call" | custom-call | tf_op jit(solution)/shard_map/attend_remote/pallas_call | solution.py:527
  70.5 2.1 %interleave_rows.1 = bf16[1024,256]{1,0:T(8,128)(2,1)} custom-call(bf16[4,256,256]{2,1,0:T(8,128)(2,1)} %attend_remote.1.in_ref), custom_call_target="tpu_custom_call" | custom-call | tf_op jit(solution)/shard_map/interleave_rows/pallas_call | solution.py:592

commit v4 on v3

--- a/solution.py
+++ b/solution.py
@@ -23,6 +23,8 @@
 ROWS = PER * CAP * CAND
 GRP = 4
 UPFRONT = 8
+BLOCKS = 4
+BROWS = 64
 
 
 def peer_of(h, low, dz, sign):
@@ -435,7 +437,7 @@
 
     def o_copy(t, d):
         there = lax.rem(me + d, NX)
-        part = pl.ds(t * 128, 128)
+        part = pl.ds(t * BROWS, BROWS)
         return pltpu.make_async_remote_copy(
             src_ref=outs.at[there, part],
             dst_ref=out_ref.at[me, part],
@@ -446,11 +448,12 @@
         )
 
     def o_own(t):
-        part = pl.ds(t * 128, 128)
+        part = pl.ds(t * BROWS, BROWS)
         return pltpu.make_async_copy(outs.at[me, part], out_ref.at[me, part], own_sem.at[t])
 
-    for t in range(2):
-        part = pl.ds(t * 128, 128)
+    kept = []
+    for t in range(BLOCKS):
+        part = pl.ds(t * BROWS, BROWS)
         full = att[part, :]
         mean = jnp.sum(full, axis=-1, keepdims=True) * (1.0 / 1024)
         var = jnp.sum(full * full, axis=-1, keepdims=True) * (1.0 / 1024) - mean * mean
@@ -463,19 +466,23 @@
             ],
             axis=1,
         )
-        for d in (2, 1, 3, 0):
+        for d in (2, 1, 3):
             there = lax.rem(me + d, NX)
             acc = csub[there, part].astype(F32) + jnp.dot(
                 gated, wo_v[there], preferred_element_type=F32
             )
-            if d:
-                outs[there, part] = acc.astype(BF16)
-                o_copy(t, d).start()
-            else:
-                outs[there, part] = acc.astype(BF16)
-                o_own(t).start()
-
-    for t in range(2):
+            outs[there, part] = acc.astype(BF16)
+            o_copy(t, d).start()
+        kept.append(gated)
+    for t in range(BLOCKS):
+        part = pl.ds(t * BROWS, BROWS)
+        acc = csub[me, part].astype(F32) + jnp.dot(
+            kept[t], wo_v[me], preferred_element_type=F32
+        )
+        outs[me, part] = acc.astype(BF16)
+        o_own(t).start()
+
+    for t in range(BLOCKS):
         o_own(t).wait()
         for d in range(1, NX):
             o_copy(t, d).wait_recv()
@@ -491,8 +498,8 @@
         pltpu.make_async_copy(part, part, x_send.at[d - 1]).wait()
         g_copy(d).wait_send()
     for d in range(1, NX):
-        o_copy(0, d).wait_send()
-        o_copy(1, d).wait_send()
+        for t in range(BLOCKS):
+            o_copy(t, d).wait_send()
 
 
 def interleave(in_ref, out_ref):
@@ -567,10 +574,10 @@
             dma((CHUNKS, 3)),
             dma,
             dma((CHUNKS,)),
-            dma((2, 3)),
-            dma((2, 3)),
+            dma((BLOCKS, 3)),
+            dma((BLOCKS, 3)),
             pltpu.SemaphoreType.REGULAR,
-            dma((2,)),
+            dma((BLOCKS,)),
         ],
         compiler_params=pltpu.CompilerParams(
             collective_id=0, has_side_effects=True, vmem_limit_bytes=56 * 1024 * 1024

time: 72.8 us -> 73 us (level)
  no operation moved by 1% of the time
where the time goes in v4:
time: 73 us; the launch traced here: 72.8 us
  Pallas kernels  72.8 us (100%)
    pallas_call x1, Pallas kernels, on_device(): pl.pallas_call(kernel, out_shape=jax.ShapeDtypeStruct((NX, REQ * SUB, 256...  70.6 us
    pallas_call x1, Pallas kernels, on_device(): pl.pallas_call(interleave, out_shape=jax.ShapeDtypeStruct((REQ * CAND, 25...  2.15 us

profile of v4, /device:TPU:1, one launch (start us, length us, event | category | flops | bytes accessed | tf_op | source)
XLA Modules:
  0.0 72.8 jit_solution(15317266804441774196)
XLA Ops:
  0.0 70.6 %attend_remote.1.in_ref = bf16[4,256,256]{2,1,0:T(8,128)(2,1)} custom-call(s32[2]{0:T(128)} %hb_ref.1, s32[1,64]{1,0:T(1,128)} %bitcast.10, s32[1,64]{1,0:T(1,128)} %bitcast.11, s32[12,64]{1,0:T(8,128)} %bitcast.8, f32[1,256]{1,0:T(1,128)} %bitcast.9, bf16[1024,1024]{1,0:T(8,128)(2,1)} %cand_hbm.1, bf16[1024,256]{1,0:T(8,128)(2,1)} %wq_hbm.1, ...), custom_call_target="tpu_custom_call" | custom-call | tf_op jit(solution)/shard_map/attend_remote/pallas_call | solution.py:534
  70.6 2.1 %interleave_rows.1 = bf16[1024,256]{1,0:T(8,128)(2,1)} custom-call(bf16[4,256,256]{2,1,0:T(8,128)(2,1)} %attend_remote.1.in_ref), custom_call_target="tpu_custom_call" | custom-call | tf_op jit(solution)/shard_map/interleave_rows/pallas_call | solution.py:599
